TPU v7x, 256 devices: a whole 4x4x8 slice. The times are simulated.
256 devices in a mesh: dp: 4 (over y_hi, core), ctx: 64 (over x, z, y_lo).
Axes of the slice: x: 4, y: 4 (y_hi: 2, y_lo: 2; y = y_hi * 2 + y_lo), z: 8, core: 2. Of those that a mesh axis runs over, the one named last changes fastest.
Arguments:
- queries: bfloat16 [32768, 1536], P(('dp', 'ctx')), parts along dimension 0, may hold values from -23 to 23
- keys: bfloat16 [32768, 128], P(('dp', 'ctx')), parts along dimension 0, may hold values from -6 to 6
- values: bfloat16 [32768, 128], P(('dp', 'ctx')), parts along dimension 0, may hold values from -6 to 6
- forward_out: bfloat16 [32768, 1536], P(('dp', 'ctx')), parts along dimension 0, may hold values from -6 to 6
- out_grad: bfloat16 [32768, 1536], P(('dp', 'ctx')), parts along dimension 0, may hold values from -24 to 24
- span_ids: int32 [512], P(('dp', 'ctx')), parts along dimension 0, may hold values from 0 to 127, as said below
Outputs:
- d_queries: bfloat16 [32768, 1536], P(('dp', 'ctx')), parts along dimension 0
- d_keys: float32 [32768, 128], P(('dp', 'ctx')), parts along dimension 0
- d_values: float32 [32768, 128], P(('dp', 'ctx')), parts along dimension 0
There are 4 independent parts, one for each index of `dp`. A program takes and returns all parts, laid end to end along the dimension named above; each array names one. Nothing has to cross between parts.
Inputs may be any that keep to these rules, and one draw needn't show every extreme that they name: `span_ids`: each span number appears once, and the two entries of one device sum to 127.
All inputs are finite; a program needn't handle non-finite values.
Results may differ from a plain program's by a relative error of at most 0.0047.
Values may be sent and summed in bfloat16 or wider, within the bound.
No kernel may reach another device: no remote copies, remote signals or barrier semaphores. Data moves between devices by JAX's collectives and lax.ppermute only.
A program may use at most 64 MiB of HBM per device.

v0:
```python
import math

import jax
import jax.numpy as jnp
from jax import lax
from jax.sharding import PartitionSpec as P

KEY_BLOCK = 512


NEG = -1e30


def head_major(block, head_count, head_width):
    row_total = block.shape[0]
    return (
        block.reshape(row_total, head_count, head_width)
        .transpose(1, 0, 2)
        .reshape(head_count * row_total, head_width)
    )


def token_major(block, head_count, head_width):
    row_total = block.shape[0] // head_count
    return (
        block.reshape(head_count, row_total, head_width)
        .transpose(1, 0, 2)
        .reshape(row_total, head_count * head_width)
    )


def masked_scores(q_rows, q_pos, k_block, k_pos, factor):
    scores = jnp.einsum("qd,kd->qk", q_rows, k_block, preferred_element_type=jnp.float32) * factor
    visible = k_pos[None, :] <= q_pos[:, None]
    return (scores, visible)


def update_statistics(row_max, row_sum, q_rows, q_pos, k_block, k_pos, factor):
    scores, visible = masked_scores(q_rows, q_pos, k_block, k_pos, factor)
    block_max = jnp.max(jnp.where(visible, scores, NEG), axis=1)
    new_max = jnp.maximum(row_max, block_max)
    shifted = jnp.where(visible, jnp.exp(scores - new_max[:, None]), 0.0)
    new_sum = row_sum * jnp.exp(row_max - new_max) + jnp.sum(shifted, axis=1)
    return (new_max, new_sum)


def score_grads(
    q_rows, g_rows, q_pos, row_max, row_sum, row_delta, k_block, v_block, k_pos, factor
):
    scores, visible = masked_scores(q_rows, q_pos, k_block, k_pos, factor)
    probs = jnp.where(visible, jnp.exp(scores - row_max[:, None]), 0.0) / row_sum[:, None]
    d_probs = jnp.einsum("qd,kd->qk", g_rows, v_block, preferred_element_type=jnp.float32)
    d_scores = (probs * (d_probs - row_delta[:, None])).astype(jnp.bfloat16)
    return (probs.astype(jnp.bfloat16), d_scores)


def key_terms(q_rows, g_rows, probs_b, d_scores):
    d_key = jnp.einsum("qk,qd->kd", d_scores, q_rows, preferred_element_type=jnp.float32)
    d_value = jnp.einsum("qk,qd->kd", probs_b, g_rows, preferred_element_type=jnp.float32)
    return jnp.concatenate([d_key, d_value], axis=1)


def per_device(queries, keys, values, forward_out, out_grad, span_ids):
    tok_rows = queries.shape[0]
    span_rows = tok_rows // 2
    head_width = keys.shape[1]
    head_count = queries.shape[1] // head_width
    factor = 1.0 / math.sqrt(head_width)
    seq_rows = tok_rows * lax.axis_size("ctx")
    span_total = 2 * lax.axis_size("ctx")
    all_ids = lax.all_gather(span_ids, "ctx", axis=0, tiled=True)
    offsets = jnp.arange(span_rows, dtype=jnp.int32)
    numbers = jnp.arange(span_total, dtype=jnp.int32)
    slot_of = jnp.sum(jnp.where(all_ids[None, :] == numbers[:, None], numbers[None, :], 0), axis=1)
    sorted_rows = (slot_of[:, None] * span_rows + offsets[None, :]).reshape(-1)
    products = (out_grad.astype(jnp.float32) * forward_out.astype(jnp.float32)).reshape(
        tok_rows, head_count, head_width
    )
    delta_all = jnp.sum(products, axis=2)
    q_list, g_list, pos_list, delta_list, last_list = ([], [], [], [], [])
    for span_slot in range(2):
        row_lower = span_slot * span_rows
        q_list.append(
            head_major(queries[row_lower : row_lower + span_rows], head_count, head_width)
        )
        g_list.append(
            head_major(out_grad[row_lower : row_lower + span_rows], head_count, head_width)
        )
        first_pos = span_ids[span_slot] * span_rows
        pos_list.append(jnp.tile(first_pos + offsets, head_count))
        delta_list.append(delta_all[row_lower : row_lower + span_rows].T.reshape(-1))
        last_list.append(first_pos + span_rows - 1)
    start_max = jnp.full((head_count * span_rows,), NEG, jnp.float32)
    start_sum = jnp.zeros((head_count * span_rows,), jnp.float32)
    gathered_keys, gathered_values = (
        lax.all_gather(keys, "ctx", axis=0, tiled=True),
        lax.all_gather(values, "ctx", axis=0, tiled=True),
    )
    sorted_keys = jnp.take(gathered_keys, sorted_rows, axis=0)
    sorted_values = jnp.take(gathered_values, sorted_rows, axis=0)
    statistics = []
    for span_slot in range(2):

        def stats_step(block_index, state, span_slot=span_slot):
            block_start = block_index * KEY_BLOCK
            k_block = lax.dynamic_slice_in_dim(sorted_keys, block_start, KEY_BLOCK, 0)
            k_pos = block_start + jnp.arange(KEY_BLOCK, dtype=jnp.int32)
            return update_statistics(
                state[0], state[1], q_list[span_slot], pos_list[span_slot], k_block, k_pos, factor
            )

        block_limit = last_list[span_slot] // KEY_BLOCK + 1
        statistics.append(lax.fori_loop(0, block_limit, stats_step, (start_max, start_sum)))

    def block_grads(span_slot, k_block, v_block, k_pos):
        return score_grads(
            q_list[span_slot],
            g_list[span_slot],
            pos_list[span_slot],
            statistics[span_slot][0],
            statistics[span_slot][1],
            delta_list[span_slot],
            k_block,
            v_block,
            k_pos,
            factor,
        )

    dq_list = []
    buffer = jnp.zeros((seq_rows, 2 * head_width), jnp.float32)
    for span_slot in range(2):

        def grad_step(block_index, state, span_slot=span_slot):
            dq_sum, grad_buffer = state
            block_start = block_index * KEY_BLOCK
            k_block = lax.dynamic_slice_in_dim(sorted_keys, block_start, KEY_BLOCK, 0)
            v_block = lax.dynamic_slice_in_dim(sorted_values, block_start, KEY_BLOCK, 0)
            k_pos = block_start + jnp.arange(KEY_BLOCK, dtype=jnp.int32)
            probs_b, d_scores = block_grads(span_slot, k_block, v_block, k_pos)
            dq_sum = dq_sum + jnp.dot(d_scores, k_block, preferred_element_type=jnp.float32)
            previous = lax.dynamic_slice_in_dim(grad_buffer, block_start, KEY_BLOCK, 0)
            fresh = key_terms(q_list[span_slot], g_list[span_slot], probs_b, d_scores)
            grad_buffer = lax.dynamic_update_slice_in_dim(
                grad_buffer, previous + fresh, block_start, 0
            )
            return (dq_sum, grad_buffer)

        block_limit = last_list[span_slot] // KEY_BLOCK + 1
        dq_start = jnp.zeros((head_count * span_rows, head_width), jnp.float32)
        dq_sum, buffer = lax.fori_loop(0, block_limit, grad_step, (dq_start, buffer))
        dq_list.append(dq_sum)
    reduced = lax.psum_scatter(buffer, "ctx", scatter_dimension=0, tiled=True)
    d_keys = reduced[:, :head_width] * factor
    d_values = reduced[:, head_width:]
    d_queries = jnp.concatenate(
        [token_major(dq_sum * factor, head_count, head_width) for dq_sum in dq_list], axis=0
    ).astype(jnp.bfloat16)
    return (d_queries, d_keys, d_values)


def solution(mesh):
    placed = (
        P(("dp", "ctx"), None),
        P(("dp", "ctx"), None),
        P(("dp", "ctx"), None),
        P(("dp", "ctx"), None),
        P(("dp", "ctx"), None),
        P(("dp", "ctx")),
    )
    return jax.shard_map(
        per_device,
        mesh=mesh,
        in_specs=placed,
        out_specs=(P(("dp", "ctx"), None), P(("dp", "ctx"), None), P(("dp", "ctx"), None)),
        check_vma=False,
    )
```

profile of v0, /device:TPU:8, one launch (start us, length us, event | category | flops | bytes accessed | tf_op | source)
XLA Modules:
  0.0 1142.4 jit_solution(16515066955509556412)
XLA Ops:
  14.1 26.2 %all-reduce = s32[128]{0:T(128)S(1)} all-reduce(s32[128]{0:T(128)S(1)} %dynamic-update-slice), channel_id=1, replica_groups=mesh['dp'=4,'ctx'=64] {'ctx'}, use_global_device_ids=true, to_apply=%add | all-reduce | flops 128 | bytes 1024
  43.9 267.3 %all-gather.5.cloned.1.call-done = bf16[8192,128]{1,0:T(8,128)(2,1)} async-done(((bf16[128,128]{1,0:T(8,128)(2,1)}), bf16[8192,128]{1,0:T(8,128)(2,1)}) %all-gather.5.cloned.1.call-update) | async-done | bytes 2097168 | tf_op jit(solution)/shard_map/all_gather | solution.py:97
  311.2 23.7 %gather_fusion.1 = bf16[8192,128]{1,0:T(8,128)(2,1)S(1)} fusion(bf16[8192,128]{1,0:T(8,128)(2,1)} %all-gather.5.cloned.1.call-done, s32[8192]{0:T(1024)S(1)} %fusion.40), kind=kCustom, calls=%fused_computation.1.clone | custom fusion | bytes 4227072 | tf_op jit(solution)/shard_map/jit(_take)/gather | solution.py:100
  335.0 275.0 %all-gather.3.cloned.1.call-done = bf16[8192,128]{1,0:T(8,128)(2,1)} async-done(((bf16[128,128]{1,0:T(8,128)(2,1)}), bf16[8192,128]{1,0:T(8,128)(2,1)}) %all-gather.3.cloned.1.call-update) | async-done | bytes 2097168 | tf_op jit(solution)/shard_map/all_gather | solution.py:96
  610.0 30.0 %gather_fusion = bf16[8192,128]{1,0:T(8,128)(2,1)} fusion(bf16[8192,128]{1,0:T(8,128)(2,1)} %all-gather.3.cloned.1.call-done, s32[8192]{0:T(1024)S(1)} %fusion.40), kind=kCustom, calls=%fused_computation.clone | custom fusion | bytes 4227072 | tf_op jit(solution)/shard_map/jit(_take)/gather | solution.py:99
  640.1 7.0 broadcast_select_fusion
  647.1 28.4 %while.54 = (s32[]{:T(128)}, f32[768]{0:T(1024)S(1)}, f32[768]{0:T(1024)S(1)}, s32[]{:T(128)}, bf16[8192,128]{1,0:T(8,128)(2,1)}, /*index=5*/bf16[768,128]{1,0:T...) while((s32[]{:T(128)}, f32[768]{0:T(1024)S(1)}, ...), condition=%wide.region_4.6_spmd.clone, body=%wide.region_1.5_spmd.clone.sunk | while | flops 103811080 | bytes 3535275 | solution.py:113
  675.6 4.2 broadcast_in_dim.64
  679.8 110.4 %while.56 = (s32[]{:T(128)}, f32[768,128]{1,0:T(8,128)S(1)}, f32[8192,256]{0,1:T(8,128)}, s32[]{:T(128)}, bf16[8192,128]{1,0:T(8,128)(2,1)}, /*index=5*/bf16[768...) while((s32[]{:T(128)}, f32[768,128]{1,0:T(8,128)S(1)}, ...), condition=%wide.wide.region_7.9_spmd.clone, body=%wide.wide.region_6.8_spmd.clone.sunk | while | flops 507216384 | bytes 11167207 | solution.py:150
  679.8 1.4 fusion.143
  682.6 1.4 convolution_add_fusion.6
  684.7 1.9 fusion.147
  686.8 1.4 fusion.143
  689.5 1.4 convolution_add_fusion.6
  691.6 1.9 fusion.147
  693.6 1.4 fusion.143
  696.4 1.4 convolution_add_fusion.6
  698.5 1.9 fusion.147
  700.5 1.4 fusion.143
  703.2 1.4 convolution_add_fusion.6
  705.4 2.0 fusion.147
  707.4 1.4 fusion.143
  710.2 1.4 convolution_add_fusion.6
  712.3 1.9 fusion.147
  714.3 1.4 fusion.143
  717.0 1.4 convolution_add_fusion.6
  719.2 1.9 fusion.147
  721.2 1.4 fusion.143
  723.9 1.4 convolution_add_fusion.6
  726.1 1.9 fusion.147
  728.1 1.4 fusion.143
  730.9 1.4 convolution_add_fusion.6
  733.0 1.9 fusion.147
  735.0 1.4 fusion.143
  737.8 1.4 convolution_add_fusion.6
  739.9 1.9 fusion.147
  741.9 1.4 fusion.143
  744.7 1.4 convolution_add_fusion.6
  746.8 1.9 fusion.147
  748.8 1.4 fusion.143
  753.7 1.9 fusion.147
  755.7 1.4 fusion.143
  758.4 1.4 convolution_add_fusion.6
  760.6 2.0 fusion.147
  762.6 1.4 fusion.143
  765.3 1.4 convolution_add_fusion.6
  767.5 1.9 fusion.147
  769.5 1.4 fusion.143
  772.2 1.4 convolution_add_fusion.6
  774.4 2.0 fusion.147
  776.4 1.4 fusion.143
  779.2 1.4 convolution_add_fusion.6
  781.3 2.0 fusion.147
  783.4 1.4 fusion.143
  786.1 1.4 convolution_add_fusion.6
  788.2 2.0 fusion.147
  790.2 1.8 while.55
  792.0 6.9 while.57
  792.1 1.4 fusion.158
  794.8 1.4 convolution_add_fusion.7
  797.0 1.9 fusion.162
  798.9 9.0 copy.38
  809.2 325.1 %reduce-scatter.2.cloned.1.call-done = f32[128,256]{1,0:T(8,128)} async-done(((f32[8192,256]{1,0:T(8,128)}), f32[128,256]{1,0:T(8,128)}) %reduce-scatter.2.cloned.1.call-update) | async-done | bytes 131088 | tf_op jit(solution)/shard_map/reduce_scatter | solution.py:152
  1134.3 1.5 fusion.43
  (294 shorter events, 76.6 us)
Async XLA Ops:
  7.2 34.8 %copy-start = (bf16[128,1536]{1,0:T(8,128)(2,1)S(1)}, bf16[128,1536]{1,0:T(8,128)(2,1)}, u32[]{:S(2)}) copy-start(bf16[128,1536]{1,0:T(8,128)(2,1)} %param.20) | copy-start | bytes 1179652
  7.2 304.1 %all-gather.5.cloned.1.call-start = ((), (), s32[]{:S(2)}) async-start(), calls=%async_computation.2 | async-start | bytes 2129920 | tf_op jit(solution)/shard_map/all_gather | solution.py:97
  7.9 602.1 %all-gather.3.cloned.1.call-start = ((), (), s32[]{:S(2)}) async-start(), calls=%async_computation.1 | async-start | bytes 2129920 | tf_op jit(solution)/shard_map/all_gather | solution.py:96
  8.7 1125.7 %reduce-scatter.2.cloned.1.call-start = ((), (), s32[]{:S(2)}) async-start(), calls=%async_computation.3 | async-start | bytes 8519680 | tf_op jit(solution)/shard_map/reduce_scatter | solution.py:152
  41.9 1.0 copy-start.1
  43.3 291.7 %copy-start.2 = (f32[12,64]{1,0:T(8,128)}, f32[12,64]{1,0:T(8,128)S(1)}, u32[]{:S(2)}) copy-start(f32[12,64]{1,0:T(8,128)S(1)} %get-tuple-element.885) | copy-start | bytes 9220
  43.3 291.7 %copy-start.3 = (f32[12,64]{1,0:T(8,128)}, f32[12,64]{1,0:T(8,128)S(1)}, u32[]{:S(2)}) copy-start(f32[12,64]{1,0:T(8,128)S(1)} %get-tuple-element.801) | copy-start | bytes 9220
Sparse Core Ops, SparseCore 0:
  9.8 301.4 all-gather.4
  313.0 296.9 all-gather.2
  808.1 326.2 reduce-scatter.1
where the time goes:
time: 1150 us; the launch traced here: 1140 us
  waiting for transfers between devices  869 us (76%)
  matrix products  104 us (9%)
  local copies, waits for them, and re-layouts  76.4 us (7%)
  other arithmetic  48.8 us (4%)
  blocking collectives  26.2 us (2%)
  between operations  16 us (1%)
    reduce_scatter x1, waiting for transfers between devices, per_device(): reduced = lax.psum_scatter(buffer, 'ctx', scatter_dimension=0, tiled=True)  325 us
    all_gather x1, waiting for transfers between devices, per_device(): lax.all_gather(keys, 'ctx', axis=0, tiled=True)  275 us
    all_gather x1, waiting for transfers between devices, per_device(): lax.all_gather(values, 'ctx', axis=0, tiled=True)  267 us
    dot_general x34, matrix products, masked_scores(): jnp.einsum('qd,kd->qk', q_rows, k_block, preferred_element_type=jnp.float32)  46.3 us
    dynamic_update_slice x17, other arithmetic, grad_step(): lax.dynamic_update_slice_in_dim(grad_buffer, previous + fresh, block_star...  33 us
    gather x1, local copies, waits for them, and re-layouts, per_device(): sorted_keys = jnp.take(gathered_keys, sorted_rows, axis=0)  30 us
    unnamed x1, blocking collectives  26.2 us
    gather x1, local copies, waits for them, and re-layouts, per_device(): sorted_values = jnp.take(gathered_values, sorted_rows, axis=0)  23.7 us
  transfers between devices with their start and end apart: 3, of which 3 were waited for; matrix products, arithmetic and copies ran while one was open for 3% of the time, Pallas kernels for 0%

commit v1 on v0

v1 whole, which is shorter than its diff:
```python
import functools
import math

import jax
import jax.numpy as jnp
from jax import lax
from jax.experimental import pallas as pl
from jax.experimental.pallas import tpu as pltpu
from jax.sharding import PartitionSpec as P

NX, NZ, NY = 4, 8, 2
DEVICES = NX * NZ * NY
SPAN = 64
SPANS = 2 * DEVICES
WIDTH = 128
HEADS = 12
ROWS = HEADS * SPAN
KINDS = 2 * NY
COLS = KINDS * ROWS
KEYS = SPANS // NY * SPAN
TILE = 4 * SPAN
CHUNK = 256
BLOCK = 2 * SPAN + 16
FACTOR = 1.0 / math.sqrt(WIDTH)
SCALE = FACTOR * math.log2(math.e)
NEG = -1e30
VMEM_LIMIT = 24 * 1024 * 1024

F32 = jnp.float32
BF16 = jnp.bfloat16


def place(x, z, y):
    return ((x % NX) * NZ + z % NZ) * NY + y % NY


def shift(block, dx=0, dz=0, dy=0):
    pairs = [
        (place(x, z, y), place(x + dx, z + dz, y + dy))
        for x in range(NX)
        for z in range(NZ)
        for y in range(NY)
    ]
    return lax.ppermute(block, "ctx", pairs)


def spans_of(meta):
    low, other = (jnp.minimum(meta[i], SPANS - 1 - meta[i]) for i in range(2))
    first, second = jnp.minimum(low, other), jnp.maximum(low, other)
    spans = (first, second, SPANS - 1 - second, SPANS - 1 - first)
    return spans, jnp.where(low < other, 0, 1)


def pick(spans, kind):
    result = spans[0]
    for i in range(1, KINDS):
        result = jnp.where(kind == i, spans[i], result)
    return result


def columns(start, width=CHUNK):
    return pl.ds(pl.multiple_of(start, WIDTH), width)


def prepare_kernel(meta, q_own, g_own, o_own, q_other, g_other, qs, gs, qt, gt, delta, products):
    spans, mine = spans_of(meta)
    delta[...] = jnp.zeros((8, COLS), F32)
    for device, (q_ref, g_ref) in enumerate(((q_own, g_own), (q_other, g_other))):
        low_kind = mine if device == 0 else 1 - mine
        for slot in range(2):
            number = meta[device] if slot == 0 else SPANS - 1 - meta[device]
            kind = jnp.where(number < DEVICES, low_kind, KINDS - 1 - low_kind)
            base = kind * ROWS
            rows = slice(slot * SPAN, (slot + 1) * SPAN)
            for b in range(HEADS // 2):
                lanes = [slice(h * WIDTH, (h + 1) * WIDTH) for h in (2 * b, 2 * b + 1)]
                q = jnp.concatenate([q_ref[rows, i] for i in lanes], axis=0)
                g = jnp.concatenate([g_ref[rows, i] for i in lanes], axis=0)
                target = columns(base + b * WIDTH, WIDTH)
                qs[target, :] = q
                gs[target, :] = g
                qt[:, target] = q.T
                gt[:, target] = g.T
                if device == 0:
                    o = jnp.concatenate([o_own[rows, i] for i in lanes], axis=0)
                    total = jnp.sum((g.astype(F32) * o.astype(F32)).T, axis=0, keepdims=True)
                    delta[:, target] = jnp.broadcast_to(total, (8, WIDTH))


def sort_spans(parts, numbers_v, numbers_s, sem, sorted_ref):
    count = 0
    for part in parts:
        for b in range(part.shape[0] // BLOCK):
            tail = part[b * BLOCK + 2 * SPAN : (b + 1) * BLOCK, :WIDTH].astype(F32)
            tail = tail.astype(jnp.int32)
            numbers_v[count : count + 1, :] = tail[0:1, :]
            numbers_v[count + 1 : count + 2, :] = tail[8:9, :]
            count += 2
    copy = pltpu.make_async_copy(numbers_v, numbers_s, sem)
    copy.start()
    copy.wait()
    first = 0
    for part in parts:
        total = part.shape[0] // BLOCK

        def step(b, carry, part=part, first=first):
            start = pl.multiple_of(b * BLOCK, 16)
            for half in range(2):
                number = numbers_s[first + 2 * b + half, 0]
                target = pl.multiple_of(number // 2 * SPAN, SPAN)
                sorted_ref[pl.ds(target, SPAN), :] = part[pl.ds(start + half * SPAN, SPAN), :]
            return carry

        lax.fori_loop(0, total, step, 0, unroll=True)
        first += 2 * total


def hidden(tile, span, parity):
    index = lax.broadcasted_iota(jnp.int32, (TILE, CHUNK), 0)
    spans = (tile * (TILE // SPAN) + index // SPAN) * NY + parity - span
    key = spans * SPAN + index % SPAN
    row = lax.broadcasted_iota(jnp.int32, (TILE, CHUNK), 1) & (SPAN - 1)
    return key > row


def last_tile(span, parity):
    return jnp.maximum(span - parity, 0) // NY // (TILE // SPAN)


def key_rows(tile):
    return pl.ds(pl.multiple_of(tile * TILE, TILE), TILE)


def statistics_kernel(n_parts, meta, *refs):
    parts = refs[:n_parts]
    qt, delta, pairs, stats, numbers_v, numbers_s, sem = refs[n_parts:]
    sort_spans(parts, numbers_v, numbers_s, sem, pairs)
    spans, _ = spans_of(meta)
    parity = meta[4]
    for kind in range(KINDS):
        span = spans[kind]
        last = last_tile(span, parity)

        def visit(tile, state, masked, kind=kind, span=span):
            k = pairs[key_rows(tile), :WIDTH]
            fresh_state = []
            for c, (before, total) in enumerate(state):
                start = kind * ROWS + c * CHUNK
                s = jnp.dot(k, qt[:, start : start + CHUNK], preferred_element_type=F32) * SCALE
                if masked:
                    s = jnp.where(hidden(tile, span, parity), 2 * NEG, s)
                s = s.reshape(TILE // 8, 8, CHUNK)
                after = jnp.maximum(before, jnp.max(s, axis=0))
                fresh = jnp.sum(jnp.exp2(s - after[None]), axis=0)
                fresh_state.append((after, total * jnp.exp2(before - after) + fresh))
            return tuple(fresh_state)

        start = (jnp.full((8, CHUNK), NEG, F32), jnp.zeros((8, CHUNK), F32))
        state = (start,) * (ROWS // CHUNK)
        state = lax.fori_loop(0, last, lambda t, s: visit(t, s, False), state)
        state = visit(last, state, True)
        for c, (row_max, row_sum) in enumerate(state):
            cols = slice(kind * ROWS + c * CHUNK, kind * ROWS + (c + 1) * CHUNK)
            top = jnp.max(row_max, axis=0, keepdims=True)
            total = jnp.sum(row_sum * jnp.exp2(row_max - top), axis=0, keepdims=True)
            stats[0:1, cols] = top
            stats[1:2, cols] = total
            stats[2:3, cols] = delta[0:1, cols]
            stats[3:8, cols] = jnp.zeros((5, CHUNK), F32)


def gradients_kernel(meta, pairs, qs, gs, qt, gt, mine_ref, other_ref, *refs):
    dq_own, dq_other = refs[:2]
    out_refs = refs[2 : 2 + NX]
    level, delta, dqt, sums = refs[2 + NX :]
    spans, mine = spans_of(meta)
    my_x, my_z, parity = meta[2], meta[3], meta[4]
    top = jnp.maximum(mine_ref[0:1, :], other_ref[0:1, :])
    total = mine_ref[1:2, :] * jnp.exp2(mine_ref[0:1, :] - top)
    total += other_ref[1:2, :] * jnp.exp2(other_ref[0:1, :] - top)
    level[...] = top + jnp.log2(total)
    delta[...] = mine_ref[2:3, :] + other_ref[2:3, :]
    dqt[...] = jnp.zeros((WIDTH, COLS), F32)
    sums[...] = jnp.zeros((KEYS, 2 * WIDTH), F32)

    def kind_step(kind, carry):
        span = pick(spans, kind)
        last = last_tile(span, parity)

        def visit(tile, masked):
            rows = key_rows(tile)
            k = pairs[rows, :WIDTH]
            v = pairs[rows, WIDTH:]
            kt = k.T
            d_key = jnp.zeros((TILE, WIDTH), F32)
            d_value = jnp.zeros((TILE, WIDTH), F32)
            for c in range(ROWS // CHUNK):
                cols = columns(kind * ROWS + c * CHUNK)
                s = jnp.dot(k, qt[:, cols], preferred_element_type=F32) * SCALE
                p = jnp.exp2(s - level[:, cols])
                if masked:
                    p = jnp.where(hidden(tile, span, parity), 0.0, p)
                dp = jnp.dot(v, gt[:, cols], preferred_element_type=F32)
                ds = (p * (dp - delta[:, cols])).astype(BF16)
                d_value += jnp.dot(p.astype(BF16), gs[cols, :], preferred_element_type=F32)
                d_key += jnp.dot(ds, qs[cols, :], preferred_element_type=F32)
                dqt[:, cols] += jnp.dot(kt, ds, preferred_element_type=F32)
            sums[rows, :WIDTH] += d_key
            sums[rows, WIDTH:] += d_value

        lax.fori_loop(0, last, lambda t, c: visit(t, False), None)
        visit(last, True)
        return carry

    lax.fori_loop(0, KINDS, kind_step, 0)

    pair = 2 * SPAN
    for x_off in range(NX):
        x = (my_x + x_off) % NX
        for z_off in range(NZ):
            z = (my_z + z_off) % NZ
            source = pl.ds(pl.multiple_of((x * NZ + z) * pair, pair), pair)
            out_refs[x_off][z_off * pair : (z_off + 1) * pair, :] = sums[source, :].astype(BF16)
    for device, out in ((0, dq_own), (1, dq_other)):
        low_kind = mine if device == 0 else 1 - mine
        for slot in range(2):
            number = meta[device] if slot == 0 else SPANS - 1 - meta[device]
            kind = jnp.where(number < DEVICES, low_kind, KINDS - 1 - low_kind)
            for b in range(ROWS // WIDTH):
                block = dqt[:, columns(kind * ROWS + b * WIDTH, WIDTH)].T * FACTOR
                for half in range(2):
                    h = 2 * b + half
                    out[slot * SPAN : (slot + 1) * SPAN, h * WIDTH : (h + 1) * WIDTH] = block[
                        half * SPAN : (half + 1) * SPAN
                    ].astype(out.dtype)


def run(kernel, meta, arrays, outs, scratch, flops, name):
    return pl.pallas_call(
        kernel,
        out_shape=[jax.ShapeDtypeStruct(s, d) for s, d in outs],
        in_specs=[pl.BlockSpec(memory_space=pltpu.SMEM)]
        + [pl.BlockSpec(memory_space=pltpu.VMEM)] * len(arrays),
        out_specs=[pl.BlockSpec(memory_space=pltpu.VMEM)] * len(outs),
        scratch_shapes=scratch,
        compiler_params=pltpu.CompilerParams(vmem_limit_bytes=VMEM_LIMIT),
        cost_estimate=pl.CostEstimate(flops=flops, bytes_accessed=10**6, transcendentals=10**6),
        name=name,
    )(meta, *arrays)


def per_device(queries, keys, values, forward_out, out_grad, span_ids):
    me = lax.axis_index("ctx")
    my_x, my_z, my_y = me // (NZ * NY), (me // NY) % NZ, me % NY
    keep_first = (span_ids[0] & 1) == my_y
    kept_number = jnp.where(keep_first, span_ids[0], span_ids[1])
    sent_number = SPANS - 1 - kept_number
    both = jnp.concatenate([keys, values], axis=1)
    upper, lower = both[:SPAN], both[SPAN:]
    kept = jnp.where(keep_first, upper, lower)
    sent = jnp.where(keep_first, lower, upper)
    rows_of = lambda n, r: jnp.broadcast_to(n.astype(BF16), (r, 2 * WIDTH))
    sent = jnp.concatenate([sent, rows_of(sent_number, 8), rows_of(span_ids[0], 8)], axis=0)
    given = shift(sent, dy=1)
    other_first = given[SPAN + 8, 0].astype(jnp.int32)
    meta = jnp.stack([span_ids[0], other_first, my_x, my_z, my_y]).astype(jnp.int32)
    q_other = shift(queries, dy=1)
    g_other = shift(out_grad, dy=1)
    block = jnp.concatenate(
        [kept, given[:SPAN], rows_of(kept_number, 8), given[SPAN : SPAN + 8]], axis=0
    )
    ring = jnp.concatenate([block] + [shift(block, dz=d) for d in range(1, NZ)], axis=0)
    parts = [ring] + [shift(ring, dx=d) for d in range(1, NX)]

    wide = ((COLS, WIDTH), BF16)
    tall = ((WIDTH, COLS), BF16)
    flat = ((8, COLS), F32)
    qs, gs, qt, gt, delta = run(
        prepare_kernel,
        meta,
        [queries, out_grad, forward_out, q_other, g_other],
        [wide, wide, tall, tall, flat],
        [pltpu.VMEM((WIDTH, WIDTH), F32)],
        10**9,
        "prepare",
    )
    pairs, stats = run(
        functools.partial(statistics_kernel, NX),
        meta,
        parts + [qt, delta],
        [((KEYS, 2 * WIDTH), BF16), flat],
        [
            pltpu.VMEM((2 * NX * NZ, WIDTH), jnp.int32),
            pltpu.SMEM((2 * NX * NZ, WIDTH), jnp.int32),
            pltpu.SemaphoreType.DMA,
        ],
        2 * 10**9,
        "row_statistics",
    )
    other_stats = shift(stats, dy=1)
    dq_own, dq_sent, *grads = run(
        gradients_kernel,
        meta,
        [pairs, qs, gs, qt, gt, stats, other_stats],
        [((2 * SPAN, HEADS * WIDTH), F32), ((2 * SPAN, HEADS * WIDTH), BF16)]
        + [((KEYS // NX, 2 * WIDTH), BF16)] * NX,
        [
            pltpu.VMEM((1, COLS), F32),
            pltpu.VMEM((1, COLS), F32),
            pltpu.VMEM((WIDTH, COLS), F32),
            pltpu.VMEM((KEYS, 2 * WIDTH), F32),
        ],
        8 * 10**9,
        "gradients",
    )

    over_x = grads[0].astype(F32)
    for d in range(1, NX):
        over_x += shift(grads[d], dx=d).astype(F32)
    over_x = over_x.astype(BF16)
    pair = 2 * SPAN
    over_z = over_x[:pair].astype(F32)
    for d in range(1, NZ):
        over_z += shift(over_x[d * pair : (d + 1) * pair], dz=d).astype(F32)
    d_queries = (dq_own + shift(dq_sent, dy=1).astype(F32)).astype(BF16)
    first = my_y == 0
    upper, lower = over_z[:SPAN], over_z[SPAN:]
    given = shift(jnp.where(first, lower, upper), dy=1)
    final = jnp.where(
        first,
        jnp.concatenate([upper, given], axis=0),
        jnp.concatenate([given, lower], axis=0),
    )
    return (d_queries, final[:, :WIDTH] * FACTOR, final[:, WIDTH:])


def solution(mesh):
    rows = P(("dp", "ctx"), None)
    return jax.shard_map(
        per_device,
        mesh=mesh,
        in_specs=(rows, rows, rows, rows, rows, P(("dp", "ctx"))),
        out_specs=(rows, rows, rows),
        check_vma=False,
    )
```

time: 1150 us -> 172 us (0.15)
  waiting for transfers between devices: 869 us -> 70.9 us
  matrix products: 104 us -> 0 us
  local copies, waits for them, and re-layouts: 76.4 us -> 7.33 us
  other arithmetic: 48.8 us -> 1.98 us
  Pallas kernels: 0 us -> 46.5 us
  starting transfers between devices: 0.11 us -> 41.2 us
  blocking collectives: 26.2 us -> 0 us
  between operations: 16 us -> 4.12 us
    all_gather x2 -> x0, waiting for transfers between devices: 542 us -> none  [the longest x1 275 us: per_device(): lax.all_gather(keys, 'ctx', axis=0, tiled=True)]
    reduce_scatter x1 -> x0, waiting for transfers between devices: 325 us -> none  [per_device(): reduced = lax.psum_scatter(buffer, 'ctx', scatter_dimension=0, tiled=True)]
    dot_general x102 -> x0, matrix products: 104 us -> none  [the longest x34 46.3 us: masked_scores(): jnp.einsum('qd,kd->qk', q_rows, k_block, preferred_element_type=jnp.float32)]
    ppermute x0 -> x26, waiting for transfers between devices: none -> 70.9 us  [shift(): return lax.ppermute(block, 'ctx', pairs)]
    gather x2 -> x0, local copies, waits for them, and re-layouts: 53.8 us -> none  [the longest x1 30 us: per_device(): sorted_keys = jnp.take(gathered_keys, sorted_rows, axis=0)]
    pallas_call x0 -> x3, Pallas kernels: none -> 46.5 us  [run(): pl.pallas_call(kernel, out_shape=[jax.ShapeDtypeStruct(s, d) for s, d in...]
    ppermute x0 -> x26, starting transfers between devices: none -> 41.2 us  [shift(): return lax.ppermute(block, 'ctx', pairs)]
    dynamic_update_slice x17 -> x0, other arithmetic: 33 us -> none  [grad_step(): lax.dynamic_update_slice_in_dim(grad_buffer, previous + fresh, block_star...]
  transfers between devices with their start and end apart: 3 -> 26, of which waited for: 3 -> 15; matrix products, arithmetic and copies ran while one was open for 3% -> 1% of each run, Pallas kernels for 0% -> 1%
where the time goes in v1:
time: 172 us
  waiting for transfers between devices  70.9 us (41%)
  Pallas kernels  46.5 us (27%)
  starting transfers between devices  41.2 us (24%)
  local copies, waits for them, and re-layouts  7.33 us (4%)
  between operations  4.12 us (2%)
  other arithmetic  1.98 us (1%)
    ppermute x26, waiting for transfers between devices, shift(): return lax.ppermute(block, 'ctx', pairs)  70.9 us
    pallas_call x3, Pallas kernels, run(): pl.pallas_call(kernel, out_shape=[jax.ShapeDtypeStruct(s, d) for s, d in...  46.5 us
    ppermute x26, starting transfers between devices, shift(): return lax.ppermute(block, 'ctx', pairs)  41.2 us
    unnamed x14, local copies, waits for them, and re-layouts  3.79 us
  transfers between devices with their start and end apart: 26, of which 15 were waited for; matrix products, arithmetic and copies ran while one was open for 1% of the time, Pallas kernels for 1%

profile of v1, /device:TPU:8, one launch (start us, length us, event | category | flops | bytes accessed | tf_op | source)
XLA Modules:
  0.0 172.0 jit_solution(16143283745339240528)
XLA Ops:
  0.6 1.3 fusion.5
  4.6 0.1 pad.9.clone
  4.7 0.1 pad.10.clone
  4.7 0.8 constant_dynamic-update-slice_fusion.1
  5.5 0.8 constant_dynamic-update-slice_fusion
  6.3 0.1 maximum_maximum_fusion
  6.4 2.3 %collective-permute-start = (bf16[80,256]{1,0:T(8,128)(2,1)S(1)}, bf16[80,256]{1,0:T(8,128)(2,1)S(1)}, u32[]{:S(2)}, u32[]{:S(2)}) collective-permute-start(bf16[80,256]{1,0:T(8,128)(2,1)S(1)} %maximum_maximum_fusion), channel_id=1, source_target_pairs={{0,1},{1,0},{2,3},{3,2},{4,5},{5,4},{6,7},{7,6},{8,9},{9,8},{10,11... | collective-permute-start | bytes 122888 | tf_op jit(solution)/shard_map/ppermute | solution.py:44
  8.7 2.0 %collective-permute-done = bf16[80,256]{1,0:T(8,128)(2,1)S(1)} collective-permute-done((bf16[80,256]{1,0:T(8,128)(2,1)S(1)}, bf16[80,256]{1,0:T(8,128)(2,1)S(1)}, u32[]{:S(2)}, u32[]{:S(2)}) %collective-permute-start) | collective-permute-done | bytes 40992 | tf_op jit(solution)/shard_map/ppermute | solution.py:44
  10.7 1.8 %collective-permute-start.1 = (bf16[144,256]{1,0:T(8,128)(2,1)S(1)}, bf16[144,256]{1,0:T(8,128)(2,1)S(1)}, u32[]{:S(2)}, u32[]{:S(2)}) collective-permute-start(bf16[144,256]{1,0:T(8,128)(2,1)S(1)} %pad_maximum_fusion), channel_id=1, source_target_pairs={{0,2},{1,3},{2,4},{3,5},{4,6},{5,7},{6,8},{7,9},{8,10},{9,11},{10,... | collective-permute-start | bytes 221192 | tf_op jit(solution)/shard_map/ppermute | solution.py:44
  12.5 4.0 %collective-permute-start.7 = (bf16[144,256]{1,0:T(8,128)(2,1)S(1)}, bf16[144,256]{1,0:T(8,128)(2,1)S(1)}, u32[]{:S(2)}, u32[]{:S(2)}) collective-permute-start(bf16[144,256]{1,0:T(8,128)(2,1)S(1)} %pad_maximum_fusion), channel_id=1, source_target_pairs={{0,14},{1,15},{2,0},{3,1},{4,2},{5,3},{6,4},{7,5},{8,6},{9,7},{10,... | collective-permute-start | bytes 221192 | tf_op jit(solution)/shard_map/ppermute | solution.py:44
  16.5 2.4 %collective-permute-start.6 = (bf16[144,256]{1,0:T(8,128)(2,1)S(1)}, bf16[144,256]{1,0:T(8,128)(2,1)S(1)}, u32[]{:S(2)}, u32[]{:S(2)}) collective-permute-start(bf16[144,256]{1,0:T(8,128)(2,1)S(1)} %pad_maximum_fusion), channel_id=1, source_target_pairs={{0,12},{1,13},{2,14},{3,15},{4,0},{5,1},{6,2},{7,3},{8,4},{9,5},{1... | collective-permute-start | bytes 221192 | tf_op jit(solution)/shard_map/ppermute | solution.py:44
  18.9 2.1 %collective-permute-start.5 = (bf16[144,256]{1,0:T(8,128)(2,1)S(1)}, bf16[144,256]{1,0:T(8,128)(2,1)S(1)}, u32[]{:S(2)}, u32[]{:S(2)}) collective-permute-start(bf16[144,256]{1,0:T(8,128)(2,1)S(1)} %pad_maximum_fusion), channel_id=1, source_target_pairs={{0,10},{1,11},{2,12},{3,13},{4,14},{5,15},{6,0},{7,1},{8,2},{9,3},... | collective-permute-start | bytes 221192 | tf_op jit(solution)/shard_map/ppermute | solution.py:44
  21.0 3.4 %collective-permute-start.4 = (bf16[144,256]{1,0:T(8,128)(2,1)S(1)}, bf16[144,256]{1,0:T(8,128)(2,1)S(1)}, u32[]{:S(2)}, u32[]{:S(2)}) collective-permute-start(bf16[144,256]{1,0:T(8,128)(2,1)S(1)} %pad_maximum_fusion), channel_id=1, source_target_pairs={{0,8},{1,9},{2,10},{3,11},{4,12},{5,13},{6,14},{7,15},{8,0},{9,1},... | collective-permute-start | bytes 221192 | tf_op jit(solution)/shard_map/ppermute | solution.py:44
  24.4 0.0 collective-permute-done.1
  24.4 7.3 %collective-permute-done.2 = bf16[144,256]{1,0:T(8,128)(2,1)S(1)} collective-permute-done((bf16[144,256]{1,0:T(8,128)(2,1)S(1)}, bf16[144,256]{1,0:T(8,128)(2,1)S(1)}, u32[]{:S(2)}, u32[]{:S(2)}) %collective-permute-start.2) | collective-permute-done | bytes 73760 | tf_op jit(solution)/shard_map/ppermute | solution.py:44
  31.7 0.4 collective-permute-start.3
  32.1 7.7 %collective-permute-done.3 = bf16[144,256]{1,0:T(8,128)(2,1)S(1)} collective-permute-done((bf16[144,256]{1,0:T(8,128)(2,1)S(1)}, bf16[144,256]{1,0:T(8,128)(2,1)S(1)}, u32[]{:S(2)}, u32[]{:S(2)}) %collective-permute-start.3) | collective-permute-done | bytes 73760 | tf_op jit(solution)/shard_map/ppermute | solution.py:44
  39.9 0.0 collective-permute-done.4
  39.9 0.0 collective-permute-done.6
  40.0 2.8 %collective-permute-start.10 = (bf16[1152,256]{1,0:T(8,128)(2,1)S(1)}, bf16[1152,256]{1,0:T(8,128)(2,1)S(1)}, u32[]{:S(2)}, u32[]{:S(2)}) collective-permute-start(bf16[1152,256]{1,0:T(8,128)(2,1)S(1)} %constant_dynamic-update-slice_fusion.2.refs_0_), channel_id=1, source_target_pairs={{0,48},{1,49},{2,50},{3,51},{4,52},{5,53},{6,54},{7,55},{8,56},{9,... | collective-permute-start | bytes 1769480 | tf_op jit(solution)/shard_map/ppermute | solution.py:44
  42.8 0.8 collective-permute-start.9
  43.6 0.9 collective-permute-start.8
  44.5 0.4 collective-permute-start.11
  44.9 1.6 collective-permute-start.12
  46.5 0.5 slice.81
  47.7 0.7 stack.23.meta
  48.4 7.0 %collective-permute-done.11.q_other = bf16[128,1536]{1,0:T(8,128)(2,1)S(1)} collective-permute-done((bf16[128,1536]{1,0:T(8,128)(2,1)}, bf16[128,1536]{1,0:T(8,128)(2,1)S(1)}, u32[]{:S(2)}, u32[]{:S(2)}) %collective-permute-start.11) | collective-permute-done | bytes 393248 | tf_op jit(solution)/shard_map/ppermute | solution.py:44
  55.4 4.2 %collective-permute-done.12.g_other = bf16[128,1536]{1,0:T(8,128)(2,1)S(1)} collective-permute-done((bf16[128,1536]{1,0:T(8,128)(2,1)}, bf16[128,1536]{1,0:T(8,128)(2,1)S(1)}, u32[]{:S(2)}, u32[]{:S(2)}) %collective-permute-start.12) | collective-permute-done | bytes 393248 | tf_op jit(solution)/shard_map/ppermute | solution.py:44
  59.6 1.0 copy-done
  60.6 1.0 copy-done.1
  61.6 1.0 copy-done.2
  62.6 1.3 prepare.1
  63.9 0.7 collective-permute-done.10.refs_3_
  64.5 3.7 %collective-permute-done.8.refs_1_ = bf16[1152,256]{1,0:T(8,128)(2,1)S(1)} collective-permute-done((bf16[1152,256]{1,0:T(8,128)(2,1)S(1)}, bf16[1152,256]{1,0:T(8,128)(2,1)S(1)}, u32[]{:S(2)}, u32[]{:S(2)}) %collective-permute-start.8) | collective-permute-done | bytes 589856 | tf_op jit(solution)/shard_map/ppermute | solution.py:44
  68.2 14.7 %row_statistics.1 = (bf16[4096,256]{1,0:T(8,128)(2,1)S(1)}, f32[8,3072]{1,0:T(8,128)S(1)}) custom-call(s32[5]{0:T(128)S(1)} %stack.23.meta, bf16[1152,256]{1,0:T(8,128)(2,1)S(1)} %constant_dynamic-update-slice_fusion.2.refs_0_, bf16[1152,256]{1,0:T(8,128)(2,1)S(1)} %collective-permute-done.8.refs_1_, bf16[1152,256]{1,0:T(8,128)(2,1)S(1)} %collective-permute-done.9.refs_2_, ...), custom_call_target="tpu_custom_call" | custom-call | flops 2000000000 | bytes 1000000 | tf_op jit(solution)/shard_map/row_statistics/pallas_call | solution.py:239
  82.9 0.9 collective-permute-start.13
  83.8 4.3 %collective-permute-done.13.other_ref = f32[8,3072]{1,0:T(8,128)S(1)} collective-permute-done((f32[8,3072]{1,0:T(8,128)S(1)}, f32[8,3072]{1,0:T(8,128)S(1)}, u32[]{:S(2)}, u32[]{:S(2)}) %collective-permute-start.13) | collective-permute-done | bytes 98336 | tf_op jit(solution)/shard_map/ppermute | solution.py:44
  88.1 30.5 %gradients.1 = (f32[128,1536]{1,0:T(8,128)S(1)}, bf16[128,1536]{1,0:T(8,128)(2,1)S(1)}, bf16[1024,256]{1,0:T(8,128)(2,1)S(1)}, bf16[1024,256]{1,0:T(8,128)(2,1)S...) custom-call(s32[5]{0:T(128)S(1)} %stack.23.meta, bf16[4096,256]{1,0:T(8,128)(2,1)S(1)} %get-tuple-element.18.pairs, ...), custom_call_target="tpu_custom_call" | custom-call | flops 8000000000 | bytes 1000000 | tf_op jit(solution)/shard_map/gradients/pallas_call | solution.py:239
  118.6 0.2 collective-permute-start.15
  118.8 2.7 %collective-permute-start.16 = (bf16[1024,256]{1,0:T(8,128)(2,1)S(1)}, bf16[1024,256]{1,0:T(8,128)(2,1)S(1)}, u32[]{:S(2)}, u32[]{:S(2)}) collective-permute-start(bf16[1024,256]{1,0:T(8,128)(2,1)S(1)} %get-tuple-element.27), channel_id=1, source_target_pairs={{0,32},{1,33},{2,34},{3,35},{4,36},{5,37},{6,38},{7,39},{8,40},{9,... | collective-permute-start | bytes 1572872 | tf_op jit(solution)/shard_map/ppermute | solution.py:44
  121.5 1.5 collective-permute-start.17
  123.0 22.6 %collective-permute-done.15 = bf16[1024,256]{1,0:T(8,128)(2,1)S(1)} collective-permute-done((bf16[1024,256]{1,0:T(8,128)(2,1)S(1)}, bf16[1024,256]{1,0:T(8,128)(2,1)S(1)}, u32[]{:S(2)}, u32[]{:S(2)}) %collective-permute-start.15) | collective-permute-done | bytes 524320 | tf_op jit(solution)/shard_map/ppermute | solution.py:44
  145.5 0.0 collective-permute-done.16
  145.5 0.6 collective-permute-done.17
  146.1 0.3 add_convert_fusion
  146.5 0.1 collective-permute-start.18
  146.6 3.2 %collective-permute-start.24 = (bf16[128,256]{1,0:T(8,128)(2,1)S(1)}, bf16[128,256]{1,0:T(8,128)(2,1)S(1)}, u32[]{:S(2)}, u32[]{:S(2)}) collective-permute-start(bf16[128,256]{1,0:T(8,128)(2,1)S(1)} %get-tuple-element.32), channel_id=1, source_target_pairs={{0,14},{1,15},{2,0},{3,1},{4,2},{5,3},{6,4},{7,5},{8,6},{9,7},{10,... | collective-permute-start | bytes 196616 | tf_op jit(solution)/shard_map/ppermute | solution.py:44
  149.8 0.0 collective-permute-start.23
  149.8 1.7 collective-permute-start.22
  151.5 4.3 %collective-permute-start.21 = (bf16[128,256]{1,0:T(8,128)(2,1)S(1)}, bf16[128,256]{1,0:T(8,128)(2,1)S(1)}, u32[]{:S(2)}, u32[]{:S(2)}) collective-permute-start(bf16[128,256]{1,0:T(8,128)(2,1)S(1)} %get-tuple-element.35), channel_id=1, source_target_pairs={{0,8},{1,9},{2,10},{3,11},{4,12},{5,13},{6,14},{7,15},{8,0},{9,1},... | collective-permute-start | bytes 196616 | tf_op jit(solution)/shard_map/ppermute | solution.py:44
  155.7 0.0 collective-permute-done.18
  155.7 0.0 collective-permute-start.20
  155.7 0.0 collective-permute-done.24
  155.7 3.7 %collective-permute-start.19 = (bf16[128,256]{1,0:T(8,128)(2,1)S(1)}, bf16[128,256]{1,0:T(8,128)(2,1)S(1)}, u32[]{:S(2)}, u32[]{:S(2)}) collective-permute-start(bf16[128,256]{1,0:T(8,128)(2,1)S(1)} %get-tuple-element.37), channel_id=1, source_target_pairs={{0,4},{1,5},{2,6},{3,7},{4,8},{5,9},{6,10},{7,11},{8,12},{9,13},{1... | collective-permute-start | bytes 196616 | tf_op jit(solution)/shard_map/ppermute | solution.py:44
  159.4 0.0 collective-permute-done.22
  159.4 2.1 %collective-permute-done.21 = bf16[128,256]{1,0:T(8,128)(2,1)S(1)} collective-permute-done((bf16[128,256]{1,0:T(8,128)(2,1)S(1)}, bf16[128,256]{1,0:T(8,128)(2,1)S(1)}, u32[]{:S(2)}, u32[]{:S(2)}) %collective-permute-start.21) | collective-permute-done | bytes 65568 | tf_op jit(solution)/shard_map/ppermute | solution.py:44
  161.6 3.2 %collective-permute-done.20 = bf16[128,256]{1,0:T(8,128)(2,1)S(1)} collective-permute-done((bf16[128,256]{1,0:T(8,128)(2,1)S(1)}, bf16[128,256]{1,0:T(8,128)(2,1)S(1)}, u32[]{:S(2)}, u32[]{:S(2)}) %collective-permute-start.20) | collective-permute-done | bytes 65568 | tf_op jit(solution)/shard_map/ppermute | solution.py:44
  164.7 2.2 %collective-permute-done.19 = bf16[128,256]{1,0:T(8,128)(2,1)S(1)} collective-permute-done((bf16[128,256]{1,0:T(8,128)(2,1)S(1)}, bf16[128,256]{1,0:T(8,128)(2,1)S(1)}, u32[]{:S(2)}, u32[]{:S(2)}) %collective-permute-start.19) | collective-permute-done | bytes 65568 | tf_op jit(solution)/shard_map/ppermute | solution.py:44
  166.9 0.1 convert_add_fusion
  167.0 0.1 collective-permute-start.25
  167.1 1.3 collective-permute-done.14
  168.4 0.8 add_convert_fusion.1
  169.3 2.1 %collective-permute-done.25 = f32[64,256]{1,0:T(8,128)S(1)} collective-permute-done((f32[64,256]{1,0:T(8,128)S(1)}, f32[64,256]{1,0:T(8,128)S(1)}, u32[]{:S(2)}, u32[]{:S(2)}) %collective-permute-start.25) | collective-permute-done | bytes 65568 | tf_op jit(solution)/shard_map/ppermute | solution.py:44
  171.4 0.7 fusion.1
  (27 shorter events, 0.2 us)
Async XLA Ops:
  6.4 4.3 %collective-permute-start = (bf16[80,256]{1,0:T(8,128)(2,1)S(1)}, bf16[80,256]{1,0:T(8,128)(2,1)S(1)}, u32[]{:S(2)}, u32[]{:S(2)}) collective-permute-start(bf16[80,256]{1,0:T(8,128)(2,1)S(1)} %maximum_maximum_fusion), channel_id=1, source_target_pairs={{0,1},{1,0},{2,3},{3,2},{4,5},{5,4},{6,7},{7,6},{8,9},{9,8},{10,11... | collective-permute-start | bytes 122888 | tf_op jit(solution)/shard_map/ppermute | solution.py:44
  10.7 13.7 %collective-permute-start.1 = (bf16[144,256]{1,0:T(8,128)(2,1)S(1)}, bf16[144,256]{1,0:T(8,128)(2,1)S(1)}, u32[]{:S(2)}, u32[]{:S(2)}) collective-permute-start(bf16[144,256]{1,0:T(8,128)(2,1)S(1)} %pad_maximum_fusion), channel_id=1, source_target_pairs={{0,2},{1,3},{2,4},{3,5},{4,6},{5,7},{6,8},{7,9},{8,10},{9,11},{10,... | collective-permute-start | bytes 221192 | tf_op jit(solution)/shard_map/ppermute | solution.py:44
  12.5 27.4 %collective-permute-start.7 = (bf16[144,256]{1,0:T(8,128)(2,1)S(1)}, bf16[144,256]{1,0:T(8,128)(2,1)S(1)}, u32[]{:S(2)}, u32[]{:S(2)}) collective-permute-start(bf16[144,256]{1,0:T(8,128)(2,1)S(1)} %pad_maximum_fusion), channel_id=1, source_target_pairs={{0,14},{1,15},{2,0},{3,1},{4,2},{5,3},{6,4},{7,5},{8,6},{9,7},{10,... | collective-permute-start | bytes 221192 | tf_op jit(solution)/shard_map/ppermute | solution.py:44
  16.5 23.4 %collective-permute-start.6 = (bf16[144,256]{1,0:T(8,128)(2,1)S(1)}, bf16[144,256]{1,0:T(8,128)(2,1)S(1)}, u32[]{:S(2)}, u32[]{:S(2)}) collective-permute-start(bf16[144,256]{1,0:T(8,128)(2,1)S(1)} %pad_maximum_fusion), channel_id=1, source_target_pairs={{0,12},{1,13},{2,14},{3,15},{4,0},{5,1},{6,2},{7,3},{8,4},{9,5},{1... | collective-permute-start | bytes 221192 | tf_op jit(solution)/shard_map/ppermute | solution.py:44
  18.9 21.0 %collective-permute-start.5 = (bf16[144,256]{1,0:T(8,128)(2,1)S(1)}, bf16[144,256]{1,0:T(8,128)(2,1)S(1)}, u32[]{:S(2)}, u32[]{:S(2)}) collective-permute-start(bf16[144,256]{1,0:T(8,128)(2,1)S(1)} %pad_maximum_fusion), channel_id=1, source_target_pairs={{0,10},{1,11},{2,12},{3,13},{4,14},{5,15},{6,0},{7,1},{8,2},{9,3},... | collective-permute-start | bytes 221192 | tf_op jit(solution)/shard_map/ppermute | solution.py:44
  21.0 18.8 %collective-permute-start.4 = (bf16[144,256]{1,0:T(8,128)(2,1)S(1)}, bf16[144,256]{1,0:T(8,128)(2,1)S(1)}, u32[]{:S(2)}, u32[]{:S(2)}) collective-permute-start(bf16[144,256]{1,0:T(8,128)(2,1)S(1)} %pad_maximum_fusion), channel_id=1, source_target_pairs={{0,8},{1,9},{2,10},{3,11},{4,12},{5,13},{6,14},{7,15},{8,0},{9,1},... | collective-permute-start | bytes 221192 | tf_op jit(solution)/shard_map/ppermute | solution.py:44
  24.4 7.3 %collective-permute-start.2 = (bf16[144,256]{1,0:T(8,128)(2,1)S(1)}, bf16[144,256]{1,0:T(8,128)(2,1)S(1)}, u32[]{:S(2)}, u32[]{:S(2)}) collective-permute-start(bf16[144,256]{1,0:T(8,128)(2,1)S(1)} %pad_maximum_fusion), channel_id=1, source_target_pairs={{0,4},{1,5},{2,6},{3,7},{4,8},{5,9},{6,10},{7,11},{8,12},{9,13},{1... | collective-permute-start | bytes 221192 | tf_op jit(solution)/shard_map/ppermute | solution.py:44
  31.7 8.1 %collective-permute-start.3 = (bf16[144,256]{1,0:T(8,128)(2,1)S(1)}, bf16[144,256]{1,0:T(8,128)(2,1)S(1)}, u32[]{:S(2)}, u32[]{:S(2)}) collective-permute-start(bf16[144,256]{1,0:T(8,128)(2,1)S(1)} %pad_maximum_fusion), channel_id=1, source_target_pairs={{0,6},{1,7},{2,8},{3,9},{4,10},{5,11},{6,12},{7,13},{8,14},{9,15},... | collective-permute-start | bytes 221192 | tf_op jit(solution)/shard_map/ppermute | solution.py:44
  40.0 24.5 %collective-permute-start.10 = (bf16[1152,256]{1,0:T(8,128)(2,1)S(1)}, bf16[1152,256]{1,0:T(8,128)(2,1)S(1)}, u32[]{:S(2)}, u32[]{:S(2)}) collective-permute-start(bf16[1152,256]{1,0:T(8,128)(2,1)S(1)} %constant_dynamic-update-slice_fusion.2.refs_0_), channel_id=1, source_target_pairs={{0,48},{1,49},{2,50},{3,51},{4,52},{5,53},{6,54},{7,55},{8,56},{9,... | collective-permute-start | bytes 1769480 | tf_op jit(solution)/shard_map/ppermute | solution.py:44
  42.8 21.7 %collective-permute-start.9 = (bf16[1152,256]{1,0:T(8,128)(2,1)S(1)}, bf16[1152,256]{1,0:T(8,128)(2,1)S(1)}, u32[]{:S(2)}, u32[]{:S(2)}) collective-permute-start(bf16[1152,256]{1,0:T(8,128)(2,1)S(1)} %constant_dynamic-update-slice_fusion.2.refs_0_), channel_id=1, source_target_pairs={{0,32},{1,33},{2,34},{3,35},{4,36},{5,37},{6,38},{7,39},{8,40},{9,... | collective-permute-start | bytes 1769480 | tf_op jit(solution)/shard_map/ppermute | solution.py:44
  43.6 24.6 %collective-permute-start.8 = (bf16[1152,256]{1,0:T(8,128)(2,1)S(1)}, bf16[1152,256]{1,0:T(8,128)(2,1)S(1)}, u32[]{:S(2)}, u32[]{:S(2)}) collective-permute-start(bf16[1152,256]{1,0:T(8,128)(2,1)S(1)} %constant_dynamic-update-slice_fusion.2.refs_0_), channel_id=1, source_target_pairs={{0,16},{1,17},{2,18},{3,19},{4,20},{5,21},{6,22},{7,23},{8,24},{9,... | collective-permute-start | bytes 1769480 | tf_op jit(solution)/shard_map/ppermute | solution.py:44
  44.5 10.9 %collective-permute-start.11 = (bf16[128,1536]{1,0:T(8,128)(2,1)}, bf16[128,1536]{1,0:T(8,128)(2,1)S(1)}, u32[]{:S(2)}, u32[]{:S(2)}) collective-permute-start(bf16[128,1536]{1,0:T(8,128)(2,1)} %q_own.1), channel_id=1, source_target_pairs={{0,1},{1,0},{2,3},{3,2},{4,5},{5,4},{6,7},{7,6},{8,9},{9,8},{10,11... | collective-permute-start | bytes 1179656 | tf_op jit(solution)/shard_map/ppermute | solution.py:44
  44.9 14.6 %collective-permute-start.12 = (bf16[128,1536]{1,0:T(8,128)(2,1)}, bf16[128,1536]{1,0:T(8,128)(2,1)S(1)}, u32[]{:S(2)}, u32[]{:S(2)}) collective-permute-start(bf16[128,1536]{1,0:T(8,128)(2,1)} %g_own.1), channel_id=1, source_target_pairs={{0,1},{1,0},{2,3},{3,2},{4,5},{5,4},{6,7},{7,6},{8,9},{9,8},{10,11... | collective-permute-start | bytes 1179656 | tf_op jit(solution)/shard_map/ppermute | solution.py:44
  59.6 1.0 copy-start
  60.6 1.0 copy-start.1
  61.6 1.0 copy-start.2
  82.9 5.2 %collective-permute-start.13 = (f32[8,3072]{1,0:T(8,128)S(1)}, f32[8,3072]{1,0:T(8,128)S(1)}, u32[]{:S(2)}, u32[]{:S(2)}) collective-permute-start(f32[8,3072]{1,0:T(8,128)S(1)} %get-tuple-element.22.mine_ref), channel_id=1, source_target_pairs={{0,1},{1,0},{2,3},{3,2},{4,5},{5,4},{6,7},{7,6},{8,9},{9,8},{10,11... | collective-permute-start | bytes 294920 | tf_op jit(solution)/shard_map/ppermute | solution.py:44
  118.6 26.9 %collective-permute-start.15 = (bf16[1024,256]{1,0:T(8,128)(2,1)S(1)}, bf16[1024,256]{1,0:T(8,128)(2,1)S(1)}, u32[]{:S(2)}, u32[]{:S(2)}) collective-permute-start(bf16[1024,256]{1,0:T(8,128)(2,1)S(1)} %get-tuple-element.26), channel_id=1, source_target_pairs={{0,16},{1,17},{2,18},{3,19},{4,20},{5,21},{6,22},{7,23},{8,24},{9,... | collective-permute-start | bytes 1572872 | tf_op jit(solution)/shard_map/ppermute | solution.py:44
  118.8 26.7 %collective-permute-start.16 = (bf16[1024,256]{1,0:T(8,128)(2,1)S(1)}, bf16[1024,256]{1,0:T(8,128)(2,1)S(1)}, u32[]{:S(2)}, u32[]{:S(2)}) collective-permute-start(bf16[1024,256]{1,0:T(8,128)(2,1)S(1)} %get-tuple-element.27), channel_id=1, source_target_pairs={{0,32},{1,33},{2,34},{3,35},{4,36},{5,37},{6,38},{7,39},{8,40},{9,... | collective-permute-start | bytes 1572872 | tf_op jit(solution)/shard_map/ppermute | solution.py:44
  121.5 24.7 %collective-permute-start.17 = (bf16[1024,256]{1,0:T(8,128)(2,1)S(1)}, bf16[1024,256]{1,0:T(8,128)(2,1)S(1)}, u32[]{:S(2)}, u32[]{:S(2)}) collective-permute-start(bf16[1024,256]{1,0:T(8,128)(2,1)S(1)} %get-tuple-element.28), channel_id=1, source_target_pairs={{0,48},{1,49},{2,50},{3,51},{4,52},{5,53},{6,54},{7,55},{8,56},{9,... | collective-permute-start | bytes 1572872 | tf_op jit(solution)/shard_map/ppermute | solution.py:44
  146.5 9.3 %collective-permute-start.18 = (bf16[128,256]{1,0:T(8,128)(2,1)S(1)}, bf16[128,256]{1,0:T(8,128)(2,1)S(1)}, u32[]{:S(2)}, u32[]{:S(2)}) collective-permute-start(bf16[128,256]{1,0:T(8,128)(2,1)S(1)} %get-tuple-element.31), channel_id=1, source_target_pairs={{0,2},{1,3},{2,4},{3,5},{4,6},{5,7},{6,8},{7,9},{8,10},{9,11},{10,... | collective-permute-start | bytes 196616 | tf_op jit(solution)/shard_map/ppermute | solution.py:44
  146.6 9.2 %collective-permute-start.24 = (bf16[128,256]{1,0:T(8,128)(2,1)S(1)}, bf16[128,256]{1,0:T(8,128)(2,1)S(1)}, u32[]{:S(2)}, u32[]{:S(2)}) collective-permute-start(bf16[128,256]{1,0:T(8,128)(2,1)S(1)} %get-tuple-element.32), channel_id=1, source_target_pairs={{0,14},{1,15},{2,0},{3,1},{4,2},{5,3},{6,4},{7,5},{8,6},{9,7},{10,... | collective-permute-start | bytes 196616 | tf_op jit(solution)/shard_map/ppermute | solution.py:44
  149.8 9.6 %collective-permute-start.23 = (bf16[128,256]{1,0:T(8,128)(2,1)S(1)}, bf16[128,256]{1,0:T(8,128)(2,1)S(1)}, u32[]{:S(2)}, u32[]{:S(2)}) collective-permute-start(bf16[128,256]{1,0:T(8,128)(2,1)S(1)} %get-tuple-element.33), channel_id=1, source_target_pairs={{0,12},{1,13},{2,14},{3,15},{4,0},{5,1},{6,2},{7,3},{8,4},{9,5},{1... | collective-permute-start | bytes 196616 | tf_op jit(solution)/shard_map/ppermute | solution.py:44
  149.8 9.6 %collective-permute-start.22 = (bf16[128,256]{1,0:T(8,128)(2,1)S(1)}, bf16[128,256]{1,0:T(8,128)(2,1)S(1)}, u32[]{:S(2)}, u32[]{:S(2)}) collective-permute-start(bf16[128,256]{1,0:T(8,128)(2,1)S(1)} %get-tuple-element.34), channel_id=1, source_target_pairs={{0,10},{1,11},{2,12},{3,13},{4,14},{5,15},{6,0},{7,1},{8,2},{9,3},... | collective-permute-start | bytes 196616 | tf_op jit(solution)/shard_map/ppermute | solution.py:44
  151.5 10.1 %collective-permute-start.21 = (bf16[128,256]{1,0:T(8,128)(2,1)S(1)}, bf16[128,256]{1,0:T(8,128)(2,1)S(1)}, u32[]{:S(2)}, u32[]{:S(2)}) collective-permute-start(bf16[128,256]{1,0:T(8,128)(2,1)S(1)} %get-tuple-element.35), channel_id=1, source_target_pairs={{0,8},{1,9},{2,10},{3,11},{4,12},{5,13},{6,14},{7,15},{8,0},{9,1},... | collective-permute-start | bytes 196616 | tf_op jit(solution)/shard_map/ppermute | solution.py:44
  155.7 9.0 %collective-permute-start.20 = (bf16[128,256]{1,0:T(8,128)(2,1)S(1)}, bf16[128,256]{1,0:T(8,128)(2,1)S(1)}, u32[]{:S(2)}, u32[]{:S(2)}) collective-permute-start(bf16[128,256]{1,0:T(8,128)(2,1)S(1)} %get-tuple-element.36), channel_id=1, source_target_pairs={{0,6},{1,7},{2,8},{3,9},{4,10},{5,11},{6,12},{7,13},{8,14},{9,15},... | collective-permute-start | bytes 196616 | tf_op jit(solution)/shard_map/ppermute | solution.py:44
  155.7 11.2 %collective-permute-start.19 = (bf16[128,256]{1,0:T(8,128)(2,1)S(1)}, bf16[128,256]{1,0:T(8,128)(2,1)S(1)}, u32[]{:S(2)}, u32[]{:S(2)}) collective-permute-start(bf16[128,256]{1,0:T(8,128)(2,1)S(1)} %get-tuple-element.37), channel_id=1, source_target_pairs={{0,4},{1,5},{2,6},{3,7},{4,8},{5,9},{6,10},{7,11},{8,12},{9,13},{1... | collective-permute-start | bytes 196616 | tf_op jit(solution)/shard_map/ppermute | solution.py:44
  159.4 9.0 %collective-permute-start.14 = (bf16[128,1536]{1,0:T(8,128)(2,1)S(1)}, bf16[128,1536]{1,0:T(8,128)(2,1)S(1)}, u32[]{:S(2)}, u32[]{:S(2)}) collective-permute-start(bf16[128,1536]{1,0:T(8,128)(2,1)S(1)} %get-tuple-element.24), channel_id=1, source_target_pairs={{0,1},{1,0},{2,3},{3,2},{4,5},{5,4},{6,7},{7,6},{8,9},{9,8},{10,11... | collective-permute-start | bytes 1179656 | tf_op jit(solution)/shard_map/ppermute | solution.py:44
  167.0 4.4 %collective-permute-start.25 = (f32[64,256]{1,0:T(8,128)S(1)}, f32[64,256]{1,0:T(8,128)S(1)}, u32[]{:S(2)}, u32[]{:S(2)}) collective-permute-start(f32[64,256]{1,0:T(8,128)S(1)} %get-tuple-element.41), channel_id=1, source_target_pairs={{0,1},{1,0},{2,3},{3,2},{4,5},{5,4},{6,7},{7,6},{8,9},{9,8},{10,11... | collective-permute-start | bytes 196616 | tf_op jit(solution)/shard_map/ppermute | solution.py:44
